TPU v7x, 256 devices: a whole 4x4x8 slice. The times are simulated.
256 devices in a mesh: pool: 2 (over core), group: 32 (over x, y, z_hi), tensor: 4 (over z_lo).
Axes of the slice: x: 4, y: 4, z: 8 (z_hi: 2, z_lo: 4; z = z_hi * 4 + z_lo), core: 2. Of those that a mesh axis runs over, the one named last changes fastest.
Arguments:
- queries: bfloat16 [2, 6144, 5120], P('pool', 'group', 'tensor'), may hold values from -8 to 8
- new_keys: bfloat16 [2, 6144, 1024], P('pool', 'group', 'tensor'), may hold values from -8 to 8
- new_values: bfloat16 [2, 6144, 1024], P('pool', 'group', 'tensor'), may hold values from -6 to 6
- cache_keys: bfloat16 [2, 32, 4096, 1024], P('pool', 'group', None, 'tensor'), may hold values from -8 to 8
- cache_values: bfloat16 [2, 32, 4096, 1024], P('pool', 'group', None, 'tensor'), may hold values from -6 to 6
- prefix_len: int32 [2, 32], P('pool', 'group'), may hold values from 1 to 4096, as said below
- span_len: int32 [2, 32], P('pool', 'group'), may hold values from 1 to 192, as said below
- residual: bfloat16 [2, 6144, 5120], P('pool', 'group', 'tensor'), may hold values from -60 to 60
- out_proj: bfloat16 [2, 5120, 5120], P('pool', 'tensor', 'group'), may hold values from -1.1953125 to 1.1953125
- norm_gain: float32 [2, 5120], P('pool', 'tensor'), may hold values from 0.5 to 1.5
Outputs:
- stream: bfloat16 [2, 6144, 5120], P('pool', 'group', 'tensor')
- normed: bfloat16 [2, 6144, 5120], P('pool', 'group', 'tensor')
Inputs may be any that keep to these rules, and one draw needn't show every extreme that they name: `prefix_len`: in each pool some sequence has exactly 4096 cached tokens. `span_len`: most spans are full; in each pool some span has 192 real tokens.
All inputs are finite; a program needn't handle non-finite values.
Results may differ from a plain program's by a relative error of at most 0.0055.
Values may be sent and summed in bfloat16 or wider, within the bound.
A program may use at most 128 MiB of HBM per device.

v0:
```python
import math

import jax
import jax.numpy as jnp
from jax import lax
from jax.sharding import PartitionSpec as P

D = 5120
H = 40
KVH = 8
HD = 128
PREFIX = 4096
SPAN = 192


epsilon = 1e-06


def from_partner(value, axis, apart):
    mask = 2**apart
    pairs = [(source, source ^ mask) for source in range(lax.axis_size(axis))]
    return lax.ppermute(value, axis, pairs)


def attend(q_block, prefix_k, prefix_v, span_k, span_v, prefix_count, span_count):
    scaling = 1.0 / math.sqrt(HD)
    prefix_scores = (
        jnp.einsum("igd,kd->gik", q_block, prefix_k, preferred_element_type=jnp.float32) * scaling
    )
    span_scores = (
        jnp.einsum("igd,kd->gik", q_block, span_k, preferred_element_type=jnp.float32) * scaling
    )
    positions = jnp.arange(PREFIX, dtype=jnp.int32)
    prefix_scores = jnp.where((positions < prefix_count)[None, None, :], prefix_scores, -jnp.inf)
    query_pos = jnp.arange(SPAN, dtype=jnp.int32)[:, None]
    key_pos = jnp.arange(SPAN, dtype=jnp.int32)[None, :]
    span_mask = (key_pos <= query_pos) & (key_pos < span_count)
    span_scores = jnp.where(span_mask[None], span_scores, -jnp.inf)
    highest = jnp.maximum(prefix_scores.max(axis=-1), span_scores.max(axis=-1))
    prefix_exp = jnp.exp(prefix_scores - highest[..., None])
    span_exp = jnp.exp(span_scores - highest[..., None])
    denominator = prefix_exp.sum(axis=-1) + span_exp.sum(axis=-1)
    numerator = jnp.einsum(
        "gik,kd->igd", prefix_exp.astype(jnp.bfloat16), prefix_v, preferred_element_type=jnp.float32
    )
    numerator = numerator + jnp.einsum(
        "gik,kd->igd", span_exp.astype(jnp.bfloat16), span_v, preferred_element_type=jnp.float32
    )
    return (numerator / jnp.transpose(denominator)[:, :, None]).astype(jnp.bfloat16)


def butterfly_out(pieces, bit_zero, along):
    first_half = jnp.take(pieces, 0, axis=along)
    second_half = jnp.take(pieces, 1, axis=along)
    return (
        jnp.where(bit_zero, second_half, first_half),
        jnp.where(bit_zero, first_half, second_half),
    )


def butterfly_in(retained, incoming, bit_zero, along):
    return jnp.where(
        bit_zero, jnp.stack([retained, incoming], along), jnp.stack([incoming, retained], along)
    )


def squares_of(tile):
    tile_float = tile.astype(jnp.float32)
    return jnp.sum(tile_float * tile_float, axis=-1)


def shards(
    queries,
    new_keys,
    new_values,
    cache_keys,
    cache_values,
    prefix_len,
    span_len,
    residual,
    out_proj,
    norm_gain,
):
    query_rows = queries[0]
    key_rows = new_keys[0]
    value_rows = new_values[0]
    past_keys = cache_keys[0]
    past_values = cache_values[0]
    group_heads = H // KVH
    local_kv = key_rows.shape[1] // HD
    seq_count = prefix_len.shape[1]

    def one_seq(seq_index):
        cached_k = past_keys[seq_index]
        cached_v = past_values[seq_index]
        prefix_count = prefix_len[0][seq_index]
        span_count = span_len[0][seq_index]

        def one_head(head_index):
            q_block = lax.dynamic_slice_in_dim(
                query_rows, head_index * group_heads * HD, group_heads * HD, 1
            )
            q_block = q_block.reshape(SPAN, group_heads, HD)

            def column_cut(source):
                return lax.dynamic_slice_in_dim(source, head_index * HD, HD, 1)

            return attend(
                q_block,
                column_cut(cached_k),
                column_cut(cached_v),
                column_cut(key_rows),
                column_cut(value_rows),
                prefix_count,
                span_count,
            )

        heads_out = lax.map(one_head, jnp.arange(local_kv, dtype=jnp.int32))
        return jnp.transpose(heads_out, (1, 0, 2, 3)).reshape(SPAN, local_kv * group_heads * HD)

    attended = lax.map(one_seq, jnp.arange(seq_count, dtype=jnp.int32))
    attended = attended.reshape(seq_count * SPAN, attended.shape[-1])
    row_count = attended.shape[0]
    local_cols = out_proj[0]
    row_slab = jnp.dot(
        lax.all_gather(attended, "group", axis=0, tiled=True),
        local_cols,
        preferred_element_type=jnp.float32,
    )
    projected = lax.psum_scatter(
        lax.all_to_all(row_slab, "group", split_axis=0, concat_axis=1, tiled=True),
        "tensor",
        scatter_dimension=1,
        tiled=True,
    )
    pool_zero = lax.axis_index("pool") == 0
    group_place = lax.axis_index("group")
    low_zero = group_place % 2 == 0
    high_zero = group_place // 2 % 2 == 0
    quarter = group_place % 4
    tile_width = projected.shape[1]
    piece_width = tile_width // 4
    own_stream = residual[0]
    summed_b = (own_stream.astype(jnp.float32) + projected).astype(jnp.bfloat16)
    outgoing = jnp.where(
        pool_zero,
        own_stream.reshape(4, row_count, piece_width),
        jnp.transpose(summed_b.reshape(row_count, 4, piece_width), (1, 0, 2)),
    )
    halves = outgoing.reshape(2, 2, row_count, piece_width)
    outbound, retained = butterfly_out(halves, low_zero, 1)
    incoming = from_partner(outbound, "group", 0)
    holding = butterfly_in(retained, incoming, low_zero, 1)
    outbound, retained = butterfly_out(holding, high_zero, 0)
    incoming = from_partner(outbound, "group", 1)
    arrived = butterfly_in(retained, incoming, high_zero, 0).reshape(4, row_count, piece_width)
    layer_first = (
        jnp.transpose(arrived, (1, 0, 2)).reshape(row_count, tile_width).astype(jnp.float32)
        + projected
    ).astype(jnp.bfloat16)
    leaving = jnp.where(pool_zero, layer_first, arrived.reshape(row_count, tile_width))
    stream_tile = from_partner(leaving, "pool", 0)
    sums_first = squares_of(stream_tile.reshape(4, row_count, piece_width))
    sums_second = jnp.broadcast_to(squares_of(stream_tile)[None], (4, row_count))
    partial_rows = jnp.where(pool_zero, sums_first, sums_second)
    tensor_rows = lax.psum(partial_rows, "tensor")
    partner_rows = tensor_rows + from_partner(tensor_rows, "group", 0)
    partner_rows = partner_rows + from_partner(partner_rows, "group", 1)
    total_rows = jnp.where(pool_zero, partner_rows, tensor_rows)
    mean_rows = total_rows / D
    tile_float = stream_tile.astype(jnp.float32)
    gain_cols = norm_gain[0]
    gain_part = lax.dynamic_slice_in_dim(gain_cols.reshape(4, piece_width), quarter, 1, 0)[0]
    scaled_first = (
        tile_float.reshape(4, row_count, piece_width)
        * lax.rsqrt(mean_rows + epsilon)[:, :, None]
        * gain_part[None, None, :]
    )
    scaled_first = scaled_first.reshape(row_count, tile_width)
    scaled_second = tile_float * lax.rsqrt(mean_rows[0] + epsilon)[:, None] * gain_cols[None, :]
    normed = jnp.where(pool_zero, scaled_first, scaled_second).astype(jnp.bfloat16)
    return (stream_tile[None], normed[None])


def solution(mesh):
    placed = (
        P("pool", "group", "tensor"),
        P("pool", "group", "tensor"),
        P("pool", "group", "tensor"),
        P("pool", "group", None, "tensor"),
        P("pool", "group", None, "tensor"),
        P("pool", "group"),
        P("pool", "group"),
        P("pool", "group", "tensor"),
        P("pool", "tensor", "group"),
        P("pool", "tensor"),
    )
    return jax.shard_map(
        shards,
        mesh=mesh,
        in_specs=placed,
        out_specs=(P("pool", "group", "tensor"), P("pool", "group", "tensor")),
        check_vma=False,
    )
```

profile of v0, /device:TPU:29, one launch (start us, length us, event | category | flops | bytes accessed | tf_op | source)
XLA Modules:
  0.0 585.5 jit_solution(16800244796720805437)
XLA Ops:
  7.2 1.3 copy.51
  8.6 59.2 %while.23 = (s32[]{:T(128)}, bf16[2,192,5,128]{3,1,2,0:T(8,128)(2,1)S(1)}, s32[2]{0:T(128)S(1)}, bf16[4096,256]{1,0:T(8,128)(2,1)}, s32[]{:T(128)}, /*index=5*/b...) while((s32[]{:T(128)}, ...), condition=%wide.region_5.6_spmd, body=%wide.region_0.5_spmd.sunk | while | flops 2152626432 | bytes 63481584 | solution.py:118
  8.6 0.6 dynamic_slice.85
  10.5 0.7 iota_compare_fusion.5
  11.2 9.1 %bitcast_reduce_fusion.2 = (f32[5,192]{1,0:T(8,128)S(1)}, f32[4096,192,5]{0,1,2:T(8,128)}) fusion(pred[4096]{0:T(1024)(128)(4,1)S(1)} %iota_compare_fusion.5, bf16[192,5,128]{0,2,1:T(8,128)(2,1)S(1)} %bitcast.150, bf16[4096,256]{1,0:T(8,128)(2,1)} %get-tuple-element.341, s32[]{:T(128)S(6)} %select_n.216), kind=kOutput, calls=%fused_computation.1.clone.1 | convolution fusion | flops 1018428480 | bytes 17030916 | tf_op jit(solution)/shard_map/while/body/eval_jaxpr/while/body/eval_jaxpr/igd,kd->gik/dot_general | solution.py:28
  20.3 0.6 iota_compare_fusion.6
  21.1 0.3 fusion.67
  21.6 9.0 %fusion.69 = f32[5,192]{1,0:T(8,128)S(1)} fusion(f32[4096,192,5]{0,1,2:T(8,128)} %get-tuple-element.300, f32[5,192]{1,0:T(8,128)S(1)} %max.11, pred[4096]{0:T(1024)(128)(4,1)S(1)} %iota_compare_fusion.5), kind=kLoop, calls=%fused_computation.4.clone.1 | loop fusion | flops 15727680 | bytes 15740416 | tf_op jit(solution)/shard_map/while/body/eval_jaxpr/while/body/eval_jaxpr/reduce_sum | solution.py:42
  30.6 7.1 %fusion.68 = f32[128,5,192]{0,2,1:T(8,128)S(1)} fusion(f32[4096,192,5]{0,1,2:T(8,128)} %get-tuple-element.300, f32[5,192]{1,0:T(8,128)S(1)} %max.11, pred[4096]{0:T(1024)(128)(4,1)S(1)} %iota_compare_fusion.5, bf16[4096,256]{1,0:T(8,128)(2,1)S(1)} %copy-done.4, s32[]{:T(128)S(6)} %select_n.216), kind=kOutput, calls=%fused_computation.6.clone.1 | convolution fusion | flops 1022361600 | bytes 17281028 | tf_op jit(solution)/shard_map/while/body/eval_jaxpr/while/body/eval_jaxpr/gik,kd->igd/dot_general | solution.py:43
  37.6 0.5 fusion.71
  38.2 0.6 dynamic_slice.85
  40.1 0.7 iota_compare_fusion.5
  40.8 9.1 %bitcast_reduce_fusion.2 = (f32[5,192]{1,0:T(8,128)S(1)}, f32[4096,192,5]{0,1,2:T(8,128)}) fusion(pred[4096]{0:T(1024)(128)(4,1)S(1)} %iota_compare_fusion.5, bf16[192,5,128]{0,2,1:T(8,128)(2,1)S(1)} %bitcast.150, bf16[4096,256]{1,0:T(8,128)(2,1)} %get-tuple-element.341, s32[]{:T(128)S(6)} %select_n.216), kind=kOutput, calls=%fused_computation.1.clone.1 | convolution fusion | flops 1018428480 | bytes 17030916 | tf_op jit(solution)/shard_map/while/body/eval_jaxpr/while/body/eval_jaxpr/igd,kd->gik/dot_general | solution.py:28
  49.9 0.6 iota_compare_fusion.6
  50.7 0.3 fusion.67
  51.2 9.0 %fusion.69 = f32[5,192]{1,0:T(8,128)S(1)} fusion(f32[4096,192,5]{0,1,2:T(8,128)} %get-tuple-element.300, f32[5,192]{1,0:T(8,128)S(1)} %max.11, pred[4096]{0:T(1024)(128)(4,1)S(1)} %iota_compare_fusion.5), kind=kLoop, calls=%fused_computation.4.clone.1 | loop fusion | flops 15727680 | bytes 15740416 | tf_op jit(solution)/shard_map/while/body/eval_jaxpr/while/body/eval_jaxpr/reduce_sum | solution.py:42
  60.1 7.1 %fusion.68 = f32[128,5,192]{0,2,1:T(8,128)S(1)} fusion(f32[4096,192,5]{0,1,2:T(8,128)} %get-tuple-element.300, f32[5,192]{1,0:T(8,128)S(1)} %max.11, pred[4096]{0:T(1024)(128)(4,1)S(1)} %iota_compare_fusion.5, bf16[4096,256]{1,0:T(8,128)(2,1)S(1)} %copy-done.4, s32[]{:T(128)S(6)} %select_n.216), kind=kOutput, calls=%fused_computation.6.clone.1 | convolution fusion | flops 1022361600 | bytes 17281028 | tf_op jit(solution)/shard_map/while/body/eval_jaxpr/while/body/eval_jaxpr/gik,kd->igd/dot_general | solution.py:43
  67.2 0.5 fusion.71
  67.7 0.2 copy.52
  68.0 1.0 copy.53
  69.1 235.0 %all-gather.2.cloned.1.call-done = bf16[6144,1280]{1,0:T(8,128)(2,1)} async-done(((bf16[192,1280]{1,0:T(8,128)(2,1)}), bf16[6144,1280]{1,0:T(8,128)(2,1)}) %all-gather.2.cloned.1.call-update) | async-done | bytes 15728656 | tf_op jit(solution)/shard_map/all_gather | solution.py:126
  304.1 8.5 %fusion.40 = f32[32,192,160]{1,2,0:T(8,128)S(1)} fusion(bf16[32,192,1280]{2,1,0:T(8,128)(2,1)} %bitcast.163, bf16[1,1280,160]{1,2,0:T(8,128)(2,1)S(1)} %copy-done), kind=kOutput, calls=%fused_computation.58 | convolution fusion | flops 2516582400 | bytes 20070400 | tf_op jit(solution)/shard_map/dot_general | solution.py:125
  312.6 84.4 %all_to_all.16 = f32[32,192,160]{1,2,0:T(8,128)} all-to-all(f32[32,192,160]{1,2,0:T(8,128)S(1)} %fusion.40), channel_id=1, replica_groups=mesh['pool'=2,'group'=32,'tensor'=4] {'group'}, dimensions={0} | all-to-all | bytes 7864320 | tf_op jit(solution)/shard_map/all_to_all | solution.py:131
  397.1 5.6 copy.54
  402.7 0.6 reshape_squeeze.6
  403.4 116.2 %reduce-scatter.2.cloned.1.call-done = f32[192,1280]{1,0:T(8,128)} async-done(((f32[192,5120]{1,0:T(8,128)}), f32[192,1280]{1,0:T(8,128)}) %reduce-scatter.2.cloned.1.call-update) | async-done | bytes 983056 | tf_op jit(solution)/shard_map/reduce_scatter | solution.py:130
  519.6 1.3 fusion.37
  520.8 0.6 reshape.120
  521.7 4.9 collective-permute-start
  526.6 8.1 %collective-permute-done = bf16[2,192,320]{2,1,0:T(8,128)(2,1)S(1)} collective-permute-done((bf16[2,192,320]{2,1,0:T(8,128)(2,1)S(1)}, bf16[2,192,320]{2,1,0:T(8,128)(2,1)S(1)}, u32[]{:S(2)}, u32[]{:S(2)}) %collective-permute-start) | collective-permute-done | bytes 245792 | tf_op jit(solution)/shard_map/ppermute | solution.py:22
  534.9 0.7 collective-permute-start.1
  535.6 6.0 %collective-permute-done.1 = bf16[2,192,320]{2,1,0:T(8,128)(2,1)S(1)} collective-permute-done((bf16[2,192,320]{2,1,0:T(8,128)(2,1)S(1)}, bf16[2,192,320]{2,1,0:T(8,128)(2,1)S(1)}, u32[]{:S(2)}, u32[]{:S(2)}) %collective-permute-start.1) | collective-permute-done | bytes 245792 | tf_op jit(solution)/shard_map/ppermute | solution.py:22
  541.9 0.5 select_n.160
  542.4 0.8 copy.58
  543.2 0.7 reshape.217
  543.9 1.3 fusion.38
  545.2 2.9 collective-permute-start.2
  548.2 1.5 collective-permute-done.2
  549.8 0.6 mul.88
  550.6 14.2 %psum.7 = f32[4,192]{1,0:T(4,128)S(1)} all-reduce(f32[4,192]{1,0:T(4,128)S(1)} %broadcast_select_fusion.2), channel_id=1, replica_groups=mesh['pool'=2,'group'=32,'tensor'=4] {'tensor'}, use_global_device_ids=true, to_apply=%region_9.14 | all-reduce | flops 768 | bytes 6144 | tf_op jit(solution)/shard_map/psum | solution.py:166
  564.9 4.5 collective-permute-start.3
  569.3 2.0 collective-permute-done.3
  571.3 0.6 collective-permute-start.4
  572.1 0.4 mul.94
  572.5 1.5 collective-permute-done.4
  574.2 1.4 mul.90
  575.6 2.2 fusion.39
  577.9 0.8 copy.73
  (51 shorter events, 2.3 us)
Async XLA Ops:
  7.2 296.9 %copy-start = (bf16[1,1280,160]{1,2,0:T(8,128)(2,1)S(1)}, bf16[1,1280,160]{1,2,0:T(8,128)(2,1)}, u32[]{:S(2)}) copy-start(bf16[1,1280,160]{1,2,0:T(8,128)(2,1)} %param.28) | copy-start | bytes 1228804
  7.2 296.9 %all-gather.2.cloned.1.call-start = ((), (), s32[]{:S(2)}) async-start(), calls=%async_computation.2 | async-start | bytes 16220160 | tf_op jit(solution)/shard_map/all_gather | solution.py:126
  8.6 12.5 %copy-start.2 = (bf16[192,256]{1,0:T(8,128)(2,1)S(1)}, bf16[192,256]{1,0:T(8,128)(2,1)}, u32[]{:S(2)}) copy-start(bf16[192,256]{1,0:T(8,128)(2,1)} %get-tuple-element.344) | copy-start | bytes 294916 | tf_op jit(solution)/shard_map/while/body/eval_jaxpr/while
  11.2 19.4 %copy-start.4 = (bf16[4096,256]{1,0:T(8,128)(2,1)S(1)}, bf16[4096,256]{1,0:T(8,128)(2,1)}, u32[]{:S(2)}) copy-start(bf16[4096,256]{1,0:T(8,128)(2,1)} %get-tuple-element.339) | copy-start | bytes 6291460 | tf_op jit(solution)/shard_map/while/body/eval_jaxpr/while
  21.6 16.1 %copy-start.5 = (bf16[192,256]{1,0:T(8,128)(2,1)S(1)}, bf16[192,256]{1,0:T(8,128)(2,1)}, u32[]{:S(2)}) copy-start(bf16[192,256]{1,0:T(8,128)(2,1)} %get-tuple-element.345) | copy-start | bytes 294916 | tf_op jit(solution)/shard_map/while/body/eval_jaxpr/while
  38.2 12.5 %copy-start.2 = (bf16[192,256]{1,0:T(8,128)(2,1)S(1)}, bf16[192,256]{1,0:T(8,128)(2,1)}, u32[]{:S(2)}) copy-start(bf16[192,256]{1,0:T(8,128)(2,1)} %get-tuple-element.344) | copy-start | bytes 294916 | tf_op jit(solution)/shard_map/while/body/eval_jaxpr/while
  40.8 19.4 %copy-start.4 = (bf16[4096,256]{1,0:T(8,128)(2,1)S(1)}, bf16[4096,256]{1,0:T(8,128)(2,1)}, u32[]{:S(2)}) copy-start(bf16[4096,256]{1,0:T(8,128)(2,1)} %get-tuple-element.339) | copy-start | bytes 6291460 | tf_op jit(solution)/shard_map/while/body/eval_jaxpr/while
  51.2 16.1 %copy-start.5 = (bf16[192,256]{1,0:T(8,128)(2,1)S(1)}, bf16[192,256]{1,0:T(8,128)(2,1)}, u32[]{:S(2)}) copy-start(bf16[192,256]{1,0:T(8,128)(2,1)} %get-tuple-element.345) | copy-start | bytes 294916 | tf_op jit(solution)/shard_map/while/body/eval_jaxpr/while
  69.0 450.5 %reduce-scatter.2.cloned.1.call-start = ((), (), s32[]{:S(2)}) async-start(), calls=%async_computation.3 | async-start | bytes 4915200 | tf_op jit(solution)/shard_map/reduce_scatter | solution.py:130
  312.6 90.1 %copy-start.1 = (bf16[1,192,1280]{2,1,0:T(8,128)(2,1)S(1)}, bf16[1,192,1280]{2,1,0:T(8,128)(2,1)}, u32[]{:S(2)}) copy-start(bf16[1,192,1280]{2,1,0:T(8,128)(2,1)} %param.27) | copy-start | bytes 1474564
  402.7 169.2 %copy-start.3 = (f32[1,1280]{1,0:T(1,128)S(1)}, f32[1,1280]{1,0:T(1,128)}, u32[]{:S(2)}) copy-start(f32[1,1280]{1,0:T(1,128)} %param.29) | copy-start | bytes 15364
  521.7 13.0 %collective-permute-start = (bf16[2,192,320]{2,1,0:T(8,128)(2,1)S(1)}, bf16[2,192,320]{2,1,0:T(8,128)(2,1)S(1)}, u32[]{:S(2)}, u32[]{:S(2)}) collective-permute-start(bf16[2,192,320]{2,1,0:T(8,128)(2,1)S(1)} %get-tuple-element.232), channel_id=1, source_target_pairs={{0,4},{4,0},{8,12},{12,8},{16,20},{20,16},{24,28},{28,24},{32,36},... | collective-permute-start | bytes 737288 | tf_op jit(solution)/shard_map/ppermute | solution.py:22
  534.9 6.7 %collective-permute-start.1 = (bf16[2,192,320]{2,1,0:T(8,128)(2,1)S(1)}, bf16[2,192,320]{2,1,0:T(8,128)(2,1)S(1)}, u32[]{:S(2)}, u32[]{:S(2)}) collective-permute-start(bf16[2,192,320]{2,1,0:T(8,128)(2,1)S(1)} %get-tuple-element.230), channel_id=1, source_target_pairs={{0,8},{4,12},{8,0},{12,4},{16,24},{20,28},{24,16},{28,20},{32,40},... | collective-permute-start | bytes 737288 | tf_op jit(solution)/shard_map/ppermute | solution.py:22
  545.2 4.4 collective-permute-start.2
  564.9 6.4 %collective-permute-start.3 = (f32[4,192]{1,0:T(4,128)S(1)}, f32[4,192]{1,0:T(4,128)S(1)}, u32[]{:S(2)}, u32[]{:S(2)}) collective-permute-start(f32[4,192]{1,0:T(4,128)S(1)} %psum.7), channel_id=1, source_target_pairs={{0,4},{4,0},{8,12},{12,8},{16,20},{20,16},{24,28},{28,24},{32,36},... | collective-permute-start | bytes 9224 | tf_op jit(solution)/shard_map/ppermute | solution.py:22
  571.3 2.8 collective-permute-start.4
Sparse Core Ops, SparseCore 0:
  69.1 234.9 all-gather.1
  402.8 116.6 reduce-scatter.1
where the time goes:
time: 590 us; the launch traced here: 585 us
  waiting for transfers between devices  370 us (63%)
  blocking collectives  98.7 us (17%)
  matrix products  42.5 us (7%)
  other arithmetic  27 us (5%)
  local copies, waits for them, and re-layouts  16.2 us (3%)
  between operations  14.2 us (2%)
  starting transfers between devices  13.7 us (2%)
    all_gather x1, waiting for transfers between devices, shards(): lax.all_gather(attended, 'group', axis=0, tiled=True)  235 us
    reduce_scatter x1, waiting for transfers between devices, shards(): lax.psum_scatter(lax.all_to_all(row_slab, 'group', split_axis=0, concat_a...  116 us
    all_to_all x1, blocking collectives, shards(): lax.all_to_all(row_slab, 'group', split_axis=0, concat_axis=1, tiled=True)  84.4 us
    ppermute x5, waiting for transfers between devices, from_partner(): return lax.ppermute(value, axis, pairs)  19 us
    dot_general x2, matrix products, attend(): jnp.einsum('igd,kd->gik', q_block, prefix_k, preferred_element_type=jnp.f...  18.3 us
    reduce_sum x4, other arithmetic, attend(): denominator = prefix_exp.sum(axis=-1) + span_exp.sum(axis=-1)  18.2 us
    psum x1, blocking collectives, shards(): tensor_rows = lax.psum(partial_rows, 'tensor')  14.2 us
    dot_general x2, matrix products, attend(): jnp.einsum('gik,kd->igd', prefix_exp.astype(jnp.bfloat16), prefix_v, pref...  14.1 us
  transfers between devices with their start and end apart: 7, of which 7 were waited for; matrix products, arithmetic and copies ran while one was open for 0% of the time, Pallas kernels for 0%

commit v1 on v0

v1 whole, which is shorter than its diff:
```python
import functools
import math

import jax
import jax.numpy as jnp
from jax import lax
from jax.experimental import pallas as pl
from jax.experimental.pallas import tpu as pltpu
from jax.sharding import PartitionSpec as P

D = 5120
HD = 128
KVL = 2
GROUP_HEADS = 5
PREFIX = 4096
SPAN = 192
ROWS = GROUP_HEADS * SPAN
HALF = GROUP_HEADS * HD
EPSILON = 1e-6
KEY_BLOCK = 2048
BLOCKS = PREFIX // KEY_BLOCK
PIECE = 320
WCOLS = 160
LOG2 = math.log2(math.e) / math.sqrt(HD)
MASKED = -1e30
MESH = pl.DeviceIdType.MESH


def nt(a, b, precision=None):
    return lax.dot_general(
        a, b, (((1,), (1,)), ((), ())), preferred_element_type=jnp.float32, precision=precision
    )


def body(
    plen_ref, slen_ref, q_hbm, k_hbm, v_hbm, sk_hbm, sv_hbm, w_hbm, res_hbm, gain_ref,
    stream_hbm, normed_hbm,
    q_ref, k_ref, v_ref, sk_ref, sv_ref,
    qs, S, Sp, mx, acc, va, vas,
    wg, ag, pr, pb, rcv1, s2, rcv2, rres, turn, lb, st, nm, sums,
    in_sem, w_loc, w_zs, w_xs, w_rs, a_ss, a_rs, res_ss, res_rs,
    p1_ss, p1_rs, p2_ss, p2_rs, f_ss, f_rs, q_ss, q_rs, out_sem,
):
    pool = lax.axis_index("pool")
    group = lax.axis_index("group")
    t = lax.axis_index("tensor")
    h = lax.rem(group, 2)
    y = lax.rem(lax.div(group, 2), 4)
    x = lax.div(group, 8)
    ylo = lax.rem(y, 2)
    yhi = lax.div(y, 2)
    zero_pool = pool == 0

    def device(px, xx, yy, hh, tt):
        return (px, (xx * 4 + yy) * 2 + hh, tt)

    def remote(src, dst, send, recv, where):
        return pltpu.make_async_remote_copy(
            src_ref=src, dst_ref=dst, send_sem=send, recv_sem=recv, device_id=where,
            device_id_type=MESH,
        )

    loads = []

    def load(src, dst, index):
        copy = pltpu.make_async_copy(src, dst, in_sem.at[index])
        copy.start()
        return copy

    load_q = load(q_hbm, q_ref, 0)
    load_sk = load(sk_hbm, sk_ref, 1)
    load_sv = load(sv_hbm, sv_ref, 2)
    load_k = [
        load(k_hbm.at[pl.ds(j * KEY_BLOCK, KEY_BLOCK)], k_ref.at[pl.ds(j * KEY_BLOCK, KEY_BLOCK)], 3 + j)
        for j in range(BLOCKS)
    ]
    load_v = load(v_hbm, v_ref, 3 + BLOCKS)

    def w_slot(hh, xx):
        return wg.at[hh, pl.ds(pl.multiple_of(xx * WCOLS, WCOLS), WCOLS)]

    z_partner = device(pool, x, y, 1 - h, t)
    x_partners = [lax.rem(x + k, 4) for k in (1, 3, 2)]
    own_w = pltpu.make_async_copy(w_hbm, w_slot(h, x), w_loc)
    own_w.start()
    w_over = remote(w_hbm, w_slot(h, x), w_zs, w_rs.at[h, x], z_partner)
    w_over.start()
    w_first = [
        remote(w_hbm, w_slot(h, x), w_xs.at[0, i], w_rs.at[h, x], device(pool, xx, y, h, t))
        for i, xx in enumerate(x_partners)
    ]
    for copy in w_first:
        copy.start()

    def w_arrival(hh, xx):
        return remote(w_slot(hh, xx), w_slot(hh, xx), w_zs, w_rs.at[hh, xx], z_partner)

    def res_plan(s):
        to_y = jnp.where(zero_pool, ylo * 2 + h, s)
        to_h = jnp.where(zero_pool, s % 2, h)
        slot = jnp.where(zero_pool, yhi * 2 + s // 2, y)
        keeps = jnp.logical_and(to_y == y, to_h == h)
        return keeps, slot, device(pool, x, to_y, to_h, t)

    def res_copies(s):
        keeps, slot, where = res_plan(s)
        near = pltpu.make_async_copy(res_hbm.at[s], rres.at[slot], res_rs.at[slot])
        far = remote(res_hbm.at[s], rres.at[slot], res_ss.at[s], res_rs.at[slot], where)
        return keeps, near, far

    for s in range(4):
        keeps, near, far = res_copies(s)

        @pl.when(keeps)
        def _():
            near.start()

        @pl.when(jnp.logical_not(keeps))
        def _():
            far.start()

    plen = plen_ref[0, 0]
    slen = slen_ref[0, 0]
    row_at = lax.broadcasted_iota(jnp.int32, (SPAN, SPAN), 0)
    col_at = lax.broadcasted_iota(jnp.int32, (SPAN, SPAN), 1)
    span_mask = (col_at <= row_at) & (col_at < slen)

    def head_rows(g):
        return slice(g * SPAN, (g + 1) * SPAN)

    def head_cols(hd, g):
        return slice((hd * GROUP_HEADS + g) * HD, (hd * GROUP_HEADS + g + 1) * HD)

    def span_scores(hd):
        for g in range(GROUP_HEADS):
            s = nt(qs[hd, head_rows(g), :], sk_ref[:, hd * HD : (hd + 1) * HD])
            s = jnp.where(span_mask, s, MASKED)
            Sp[hd, head_rows(g), :] = s
            rest = s[:, HD:]
            mx[hd, head_rows(g), :] = jnp.maximum(
                s[:, :HD], jnp.concatenate([rest, rest], axis=1)
            )

    def scores(hd, j):
        base = pl.multiple_of(j * KEY_BLOCK, KEY_BLOCK)
        keys = k_ref[pl.ds(base, KEY_BLOCK), hd * HD : (hd + 1) * HD]
        position = base + lax.broadcasted_iota(jnp.int32, (1, KEY_BLOCK), 1)
        bias = jnp.where(position < plen, 0.0, MASKED)
        slot = lax.rem(hd * BLOCKS + j, 3)
        for g in range(GROUP_HEADS):
            s = nt(qs[hd, head_rows(g), :], keys) + bias
            S[slot, head_rows(g), :] = s
            m = mx[hd, head_rows(g), :]
            for u in range(0, KEY_BLOCK, HD):
                m = jnp.maximum(m, s[:, u : u + HD])
            mx[hd, head_rows(g), :] = m

    def finish_max(hd):
        m = jnp.max(mx[hd], axis=1, keepdims=True) * LOG2
        mx[hd] = jnp.broadcast_to(m, (ROWS, HD))

    def weigh(hd, j):
        base = pl.multiple_of(j * KEY_BLOCK, KEY_BLOCK)
        values = va[hd, pl.ds(base, KEY_BLOCK), :]
        slot = lax.rem(hd * BLOCKS + j, 3)
        for g in range(GROUP_HEADS):
            m = mx[hd, head_rows(g), :]
            wide = jnp.concatenate([m] * (KEY_BLOCK // HD), axis=1)
            p = jnp.exp2(S[slot, head_rows(g), :] * LOG2 - wide).astype(jnp.bfloat16)
            acc[hd, head_rows(g), :] += jnp.dot(p, values, preferred_element_type=jnp.float32)

    def span_weigh(hd):
        for g in range(GROUP_HEADS):
            m = mx[hd, head_rows(g), :]
            wide = jnp.concatenate([m, m[:, : SPAN - HD]], axis=1)
            p = jnp.exp2(Sp[hd, head_rows(g), :] * LOG2 - wide).astype(jnp.bfloat16)
            acc[hd, head_rows(g), :] = jnp.dot(p, vas[hd], preferred_element_type=jnp.float32)

    def a_slot(hd, yy):
        return ag.at[hd, pl.ds(pl.multiple_of(yy * SPAN, SPAN), SPAN)]

    def attended(hd):
        for g in range(GROUP_HEADS):
            a = acc[hd, head_rows(g), :]
            out = (a[:, :HD] / a[:, HD:]).astype(jnp.bfloat16)
            ag[hd, pl.ds(pl.multiple_of(y * SPAN, SPAN), SPAN), g * HD : (g + 1) * HD] = out

    y_partners = [yhi * 2 + 1 - ylo, (1 - yhi) * 2 + ylo, (1 - yhi) * 2 + 1 - ylo]

    def a_copies(hd):
        return [
            remote(a_slot(hd, y), a_slot(hd, y), a_ss.at[hd, i], a_rs.at[hd, y], device(pool, x, yy, h, t))
            for i, yy in enumerate(y_partners)
        ]

    def a_arrival(hd, yy):
        return remote(a_slot(hd, yy), a_slot(hd, yy), a_ss.at[hd, 0], a_rs.at[hd, yy], z_partner)

    load_q.wait()
    for hd in range(KVL):
        for g in range(GROUP_HEADS):
            qs[hd, head_rows(g), :] = q_ref[:, head_cols(hd, g)]
    load_sk.wait()
    span_scores(0)
    for copy in load_k:
        copy.wait()
    pl.loop(0, BLOCKS)(lambda j: scores(0, j))
    load_v.wait()
    load_sv.wait()
    for hd in range(KVL):
        va[hd, :, :HD] = v_ref[:, hd * HD : (hd + 1) * HD]
        va[hd, :, HD:] = jnp.ones((PREFIX, HD), jnp.bfloat16)
        vas[hd, :, :HD] = sv_ref[:, hd * HD : (hd + 1) * HD]
        vas[hd, :, HD:] = jnp.ones((SPAN, HD), jnp.bfloat16)
    finish_max(0)
    span_weigh(0)
    span_scores(1)

    def middle(j):
        weigh(0, j)
        scores(1, j)

    pl.loop(0, BLOCKS)(middle)
    attended(0)
    first_a = a_copies(0)
    for copy in first_a:
        copy.start()
    finish_max(1)
    span_weigh(1)
    pl.loop(0, BLOCKS)(lambda j: weigh(1, j))
    attended(1)
    second_a = a_copies(1)
    for copy in second_a:
        copy.start()

    w_arrival(1 - h, x).wait_recv()
    w_second = [
        remote(
            w_slot(1 - h, x), w_slot(1 - h, x), w_xs.at[1, i], w_rs.at[1 - h, x], device(pool, xx, y, h, t)
        )
        for i, xx in enumerate(x_partners)
    ]
    for copy in w_second:
        copy.start()

    t1 = t + 1 - 2 * lax.rem(t, 2)
    t2 = lax.rem(t + 2, 4)
    t3 = 3 - t
    tpar = lax.rem(t, 2)
    thi = lax.div(t, 2)

    def piece_rows(piece):
        return pl.ds(pl.multiple_of(piece * WCOLS, WCOLS), WCOLS)

    def p1_copy(u, i, piece):
        return remote(
            pb.at[u, piece_rows(piece)], rcv1.at[lax.div(piece, 2), u], p1_ss.at[u, i],
            p1_rs.at[lax.div(piece, 2), u], device(pool, x, y, h, t1),
        )

    def p1_arrival(jj, u):
        return remote(rcv1.at[jj, u], rcv1.at[jj, u], p1_ss.at[u, 0], p1_rs.at[jj, u], z_partner)

    def p2_copy(u):
        return remote(s2.at[u], rcv2.at[u], p2_ss.at[u], p2_rs.at[u], device(pool, x, y, h, t2))

    def unit(u):
        hh = h if u < 2 else 1 - h
        pair = yhi if u % 2 == 0 else 1 - yhi
        rows = pl.ds(pl.multiple_of(pair * 2 * SPAN, 2 * SPAN), 2 * SPAN)
        total = nt(wg[hh, :, :HALF], ag[0, rows, :]) + nt(wg[hh, :, HALF:], ag[1, rows, :])
        pr[u] = total
        pb[u] = total.astype(jnp.bfloat16)
        sent = [p1_copy(u, 0, t3), p1_copy(u, 1, t1)]
        for copy in sent:
            copy.start()
        return sent

    def second(u):
        p1_arrival(1 - thi, u).wait_recv()
        total = pr[u, piece_rows(t2), :] + rcv1[1 - thi, u].astype(jnp.float32)
        s2[u] = total.astype(jnp.bfloat16)
        copy = p2_copy(u)
        copy.start()
        return copy

    p1_sent = []
    p2_sent = []
    own_w.wait()
    for xx in x_partners:
        w_arrival(h, xx).wait_recv()
    for hd in range(KVL):
        a_arrival(hd, y_partners[0]).wait_recv()
    p1_sent += unit(0)
    for hd in range(KVL):
        for yy in y_partners[1:]:
            a_arrival(hd, yy).wait_recv()
    p1_sent += unit(1)
    p2_sent.append(second(0))
    for xx in x_partners:
        w_arrival(1 - h, xx).wait_recv()
    p1_sent += unit(2)
    p2_sent.append(second(1))
    p1_sent += unit(3)
    p2_sent.append(second(2))
    p2_sent.append(second(3))

    def final_copy(s, slot_from, index):
        to_y = jnp.where(zero_pool, s, lax.div(s, 2) * 2 + yhi)
        to_h = jnp.where(zero_pool, h, ylo)
        slot = jnp.where(zero_pool, y, lax.rem(s, 2) * 2 + h)
        return remote(
            lb.at[slot_from], st.at[slot], f_ss.at[index], f_rs.at[slot],
            device(1 - pool, x, to_y, to_h, t),
        )

    turn[pl.ds(PIECE, 64), :] = jnp.zeros((64, 2 * SPAN), jnp.float32)
    final_sent = []
    for pp in range(2):
        pair = yhi if pp == 0 else 1 - yhi
        for hh in range(2):
            u = hh * 2 + pp
            at = h if hh == 0 else 1 - h
            p1_arrival(thi, u).wait_recv()
            p2_copy(u).wait_recv()
            total = (
                pr[u, piece_rows(t), :]
                + rcv1[thi, u].astype(jnp.float32)
                + rcv2[u].astype(jnp.float32)
            )
            turn[pl.ds(pl.multiple_of(at * WCOLS, WCOLS), WCOLS), :] = total
        whole = jnp.transpose(turn[...])[:, :PIECE]
        for a in range(2):
            s = pair * 2 + a
            pltpu.make_async_copy(rres.at[s], rres.at[s], res_rs.at[s]).wait()
            out = whole[a * SPAN : (a + 1) * SPAN] + rres[s].astype(jnp.float32)
            lb[pp * 2 + a] = out.astype(jnp.bfloat16)
            copy = final_copy(s, pp * 2 + a, pp * 2 + a)
            copy.start()
            final_sent.append(copy)

    own_index = (ylo * 2 + h) * 4 + t
    ones = jnp.ones((8, PIECE), jnp.float32)
    row_sums = []
    for s in range(4):
        remote(lb.at[s], st.at[s], f_ss.at[s], f_rs.at[s], z_partner).wait_recv()
        tile = st[s].astype(jnp.float32)
        row_sums.append(nt(ones, tile * tile, lax.Precision.HIGHEST))
    stream_out = pltpu.make_async_copy(st, stream_hbm, out_sem.at[0])
    stream_out.start()
    across = row_sums[0] + row_sums[1] + row_sums[2] + row_sums[3]
    sub = lax.broadcasted_iota(jnp.int32, (8, SPAN), 0)
    mine = jnp.zeros((8, SPAN), jnp.float32)
    for s in range(4):
        mine = jnp.where(sub == s, row_sums[s], mine)
    mine = jnp.where(zero_pool, mine, across)
    sums[own_index, :, :SPAN] = mine
    sums[own_index, :, SPAN:] = jnp.zeros((8, 256 - SPAN), jnp.float32)
    sum_sent = []
    for k in range(1, 16):
        to_y = yhi * 2 + lax.rem(ylo + k // 8, 2)
        to_h = lax.rem(h + (k // 4) % 2, 2)
        to_t = lax.rem(t + k % 4, 4)
        copy = remote(
            sums.at[own_index], sums.at[own_index], q_ss.at[k], q_rs.at[own_index],
            device(pool, x, to_y, to_h, to_t),
        )
        copy.start()
        sum_sent.append(copy)
    total = mine
    for k in range(1, 16):
        from_y = lax.rem(ylo + k // 8, 2)
        from_h = lax.rem(h + (k // 4) % 2, 2)
        index = (from_y * 2 + from_h) * 4 + lax.rem(t + k % 4, 4)
        remote(sums.at[index], sums.at[index], q_ss.at[k], q_rs.at[index], z_partner).wait_recv()
        part = sums[index, :, :SPAN]
        if k >= 4:
            part = jnp.where(zero_pool, part, 0.0)
        total = total + part
    scale = lax.rsqrt(total * (1.0 / D) + EPSILON)
    for s in range(4):
        picked = jnp.where(sub == s, scale, 0.0)
        wide = lax.dot_general(
            picked, ones, (((0,), (0,)), ((), ())), preferred_element_type=jnp.float32,
            precision=lax.Precision.HIGHEST,
        )
        gain_at = jnp.where(zero_pool, ylo * 2 + h, s)
        gain = gain_ref[pl.ds(gain_at, 1), :]
        nm[s] = (st[s].astype(jnp.float32) * wide * gain).astype(jnp.bfloat16)
    normed_out = pltpu.make_async_copy(nm, normed_hbm, out_sem.at[1])
    normed_out.start()

    w_over.wait_send()
    for copy in w_first + w_second + first_a + second_a + p1_sent + p2_sent + final_sent + sum_sent:
        copy.wait_send()
    for s in range(4):
        keeps, near, far = res_copies(s)

        @pl.when(jnp.logical_not(keeps))
        def _():
            far.wait_send()

    stream_out.wait()
    normed_out.wait()


def fused(plen, slen, q, k, v, sk, sv, w, res, gain):
    smem = pl.BlockSpec(memory_space=pltpu.SMEM)
    vmem = pl.BlockSpec(memory_space=pltpu.VMEM)
    hbm = pl.BlockSpec(memory_space=pl.ANY)
    dma = pltpu.SemaphoreType.DMA
    bf, f32 = jnp.bfloat16, jnp.float32
    out = jax.ShapeDtypeStruct((4, SPAN, PIECE), bf)
    return pl.pallas_call(
        body,
        out_shape=(out, out),
        in_specs=[smem, smem] + [hbm] * 7 + [vmem],
        out_specs=(hbm, hbm),
        scratch_shapes=[
            pltpu.VMEM((SPAN, 2 * HALF), bf),
            pltpu.VMEM((PREFIX, KVL * HD), bf),
            pltpu.VMEM((PREFIX, KVL * HD), bf),
            pltpu.VMEM((SPAN, KVL * HD), bf),
            pltpu.VMEM((SPAN, KVL * HD), bf),
            pltpu.VMEM((KVL, ROWS, HD), bf),
            pltpu.VMEM((3, ROWS, KEY_BLOCK), f32),
            pltpu.VMEM((KVL, ROWS, SPAN), f32),
            pltpu.VMEM((KVL, ROWS, HD), f32),
            pltpu.VMEM((KVL, ROWS, 2 * HD), f32),
            pltpu.VMEM((KVL, PREFIX, 2 * HD), bf),
            pltpu.VMEM((KVL, SPAN, 2 * HD), bf),
            pltpu.VMEM((2, 4 * WCOLS, 2 * HALF), bf),
            pltpu.VMEM((KVL, 4 * SPAN, HALF), bf),
            pltpu.VMEM((4, 4 * WCOLS, 2 * SPAN), f32),
            pltpu.VMEM((4, 4 * WCOLS, 2 * SPAN), bf),
            pltpu.VMEM((2, 4, WCOLS, 2 * SPAN), bf),
            pltpu.VMEM((4, WCOLS, 2 * SPAN), bf),
            pltpu.VMEM((4, WCOLS, 2 * SPAN), bf),
            pltpu.VMEM((4, SPAN, PIECE), bf),
            pltpu.VMEM((PIECE + 64, 2 * SPAN), f32),
            pltpu.VMEM((4, SPAN, PIECE), bf),
            pltpu.VMEM((4, SPAN, PIECE), bf),
            pltpu.VMEM((4, SPAN, PIECE), bf),
            pltpu.VMEM((16, 8, 256), f32),
            dma((4 + BLOCKS,)),
            dma,
            dma,
            dma((2, 3)),
            dma((2, 4)),
            dma((KVL, 3)),
            dma((KVL, 4)),
            dma((4,)),
            dma((4,)),
            dma((4, 2)),
            dma((2, 4)),
            dma((4,)),
            dma((4,)),
            dma((4,)),
            dma((4,)),
            dma((16,)),
            dma((16,)),
            dma((2,)),
        ],
        compiler_params=pltpu.CompilerParams(has_side_effects=True, vmem_limit_bytes=60 << 20),
        name="fused",
    )(plen, slen, q, k, v, sk, sv, w, res, gain)


def shards(
    queries, new_keys, new_values, cache_keys, cache_values, prefix_len, span_len, residual, out_proj,
    norm_gain,
):
    zero_pool = lax.axis_index("pool") == 0
    own = residual[0]
    pieces = jnp.where(
        zero_pool,
        own.reshape(4, SPAN, PIECE),
        jnp.transpose(own.reshape(SPAN, 4, PIECE), (1, 0, 2)),
    )
    stream, normed = fused(
        prefix_len, span_len, queries[0], cache_keys[0, 0], cache_values[0, 0], new_keys[0],
        new_values[0], jnp.swapaxes(out_proj[0], 0, 1), pieces, norm_gain[0].reshape(4, PIECE),
    )

    def whole(four):
        return jnp.where(
            zero_pool,
            four.reshape(SPAN, 4 * PIECE),
            jnp.transpose(four, (1, 0, 2)).reshape(SPAN, 4 * PIECE),
        )

    return whole(stream)[None], whole(normed)[None]


def solution(mesh):
    placed = (
        P("pool", "group", "tensor"),
        P("pool", "group", "tensor"),
        P("pool", "group", "tensor"),
        P("pool", "group", None, "tensor"),
        P("pool", "group", None, "tensor"),
        P("pool", "group"),
        P("pool", "group"),
        P("pool", "group", "tensor"),
        P("pool", "tensor", "group"),
        P("pool", "tensor"),
    )
    return jax.shard_map(
        shards,
        mesh=mesh,
        in_specs=placed,
        out_specs=(P("pool", "group", "tensor"), P("pool", "group", "tensor")),
        check_vma=False,
    )
```

time: 590 us -> 122 us (0.21)
  waiting for transfers between devices: 370 us -> 0 us
  Pallas kernels: 0 us -> 107 us
  blocking collectives: 98.7 us -> 0 us
  matrix products: 42.5 us -> 0 us
  other arithmetic: 27 us -> 1.98 us
  starting transfers between devices: 13.7 us -> 0 us
  between operations: 14.2 us -> 2.02 us
  local copies, waits for them, and re-layouts: 16.2 us -> 9.15 us
    all_gather x1 -> x0, waiting for transfers between devices: 235 us -> none  [shards(): lax.all_gather(attended, 'group', axis=0, tiled=True)]
    reduce_scatter x1 -> x0, waiting for transfers between devices: 116 us -> none  [shards(): lax.psum_scatter(lax.all_to_all(row_slab, 'group', split_axis=0, concat_a...]
    pallas_call x0 -> x1, Pallas kernels: none -> 107 us  [fused(): pl.pallas_call(body, out_shape=(out, out), in_specs=[smem, smem] + [hbm]...]
    all_to_all x1 -> x0, blocking collectives: 84.4 us -> none  [shards(): lax.all_to_all(row_slab, 'group', split_axis=0, concat_axis=1, tiled=True)]
    dot_general x9 -> x0, matrix products: 42.5 us -> none  [the longest x2 18.3 us: attend(): jnp.einsum('igd,kd->gik', q_block, prefix_k, preferred_element_type=jnp.f...]
    ppermute x5 -> x0, waiting for transfers between devices: 19 us -> none  [from_partner(): return lax.ppermute(value, axis, pairs)]
    reduce_sum x6 -> x0, other arithmetic: 18.6 us -> none  [the longest x4 18.2 us: attend(): denominator = prefix_exp.sum(axis=-1) + span_exp.sum(axis=-1)]
    psum x1 -> x0, blocking collectives: 14.2 us -> none  [shards(): tensor_rows = lax.psum(partial_rows, 'tensor')]
  transfers between devices with their start and end apart: 7 -> 0, of which waited for: 7 -> 0; matrix products, arithmetic and copies ran while one was open for 0% -> 0% of each run, Pallas kernels for 0% -> 0%
where the time goes in v1:
time: 122 us; the launch traced here: 120 us
  Pallas kernels  107 us (88%)
  local copies, waits for them, and re-layouts  9.15 us (8%)
  between operations  2.02 us (2%)
  other arithmetic  1.98 us (2%)
    pallas_call x1, Pallas kernels, fused(): pl.pallas_call(body, out_shape=(out, out), in_specs=[smem, smem] + [hbm]...  107 us

profile of v1, /device:TPU:29, one launch (start us, length us, event | category | flops | bytes accessed | tf_op | source)
XLA Modules:
  0.0 120.0 jit_solution(3047445804581421448)
XLA Ops:
  0.6 0.0 copy-start.1
  1.9 1.7 %reshape_squeeze.9 = bf16[4,192,320]{2,1,0:T(8,128)(2,1)S(1)} reshape(bf16[1,192,1280]{2,1,0:T(8,128)(2,1)} %param.17) | data formatting | bytes 983040 | tf_op jit(solution)/shard_map/reshape;squeeze | solution.py:477
  3.6 1.7 %reshape_squeeze.10 = bf16[192,4,320]{2,1,0:T(4,128)(2,1)S(1)} reshape(bf16[1,192,1280]{2,1,0:T(8,128)(2,1)} %param.17) | data formatting | bytes 983040 | tf_op jit(solution)/shard_map/reshape;squeeze | solution.py:478
  5.3 0.9 bitcast_select_fusion.res_hbm
  6.3 0.0 copy-done.1
  6.3 0.7 reshape_squeeze.11.gain_ref
  7.0 106.8 %fused.1 = (bf16[4,192,320]{2,1,0:T(8,128)(2,1)}, bf16[4,192,320]{2,1,0:T(8,128)(2,1)}) custom-call(s32[1,1]{1,0:T(1,128)S(6)} %copy.16.plen_ref, s32[1,1]{1,0:T(1,128)S(6)} %copy.17.slen_ref, bf16[192,1280]{1,0:T(8,128)(2,1)} %bitcast.16, bf16[4096,256]{1,0:T(8,128)(2,1)} %bitcast.14, bf16[4096,256]{1,0:T(8,128)(2,1)} %bitcast.15, ...), custom_call_target="tpu_custom_call" | custom-call | tf_op jit(solution)/shard_map/fused/pallas_call | solution.py:414
  113.8 0.0 copy-start
  113.8 1.7 %reshape.52 = bf16[1,192,1280]{2,1,0:T(8,128)(2,1)S(1)} reshape(bf16[4,192,320]{2,1,0:T(8,128)(2,1)} %get-tuple-element.5) | data formatting | bytes 983040 | tf_op jit(solution)/shard_map/reshape | solution.py:488
  115.5 1.5 %copy.14 = bf16[192,4,320]{2,1,0:T(4,128)(2,1)S(1)} copy(bf16[192,4,320]{2,0,1:T(8,128)(2,1)} %bitcast.13) | data formatting | bytes 983040 | tf_op jit(solution)/shard_map/transpose | solution.py:489
  117.0 0.5 reshape.53
  117.4 0.0 copy-done
  117.5 0.5 reshape.50
  118.0 0.5 copy.13
  118.4 0.5 reshape.51
  118.9 1.0 broadcast_select_fusion
  (1 shorter events, 0.0 us)
Async XLA Ops:
  0.6 5.6 %copy-start.1 = (f32[1,1280]{1,0:T(1,128)S(1)}, f32[1,1280]{1,0:T(1,128)}, u32[]{:S(2)}) copy-start(f32[1,1280]{1,0:T(1,128)} %param.19) | copy-start | bytes 15364
  113.8 3.7 %copy-start = (bf16[4,192,320]{2,1,0:T(8,128)(2,1)S(1)}, bf16[4,192,320]{2,1,0:T(8,128)(2,1)}, u32[]{:S(2)}) copy-start(bf16[4,192,320]{2,1,0:T(8,128)(2,1)} %get-tuple-element.4) | copy-start | bytes 1474564
